TPU v7x, 256 devices: a whole 4x4x8 slice. The times are simulated.
256 devices in a mesh: dp: 16 (over y, x), tensor: 16 (over z, core).
Axes of the slice: x: 4, y: 4, z: 8, core: 2. Of those that a mesh axis runs over, the one named last changes fastest.
Arguments:
- inputs: bfloat16 [12288, 4096], P('dp', 'tensor'), may hold values from -6 to 6
- cotangent: bfloat16 [12288, 4096], P('dp', 'tensor'), may hold values from -0.059814453 to 0.059814453
- gate_pre: bfloat16 [12288, 18432], P('dp', 'tensor'), may hold values from -6 to 6
- up_pre: bfloat16 [12288, 18432], P('dp', 'tensor'), may hold values from -6 to 6
- down_weight: bfloat16 [18432, 4096], P('tensor'), may hold values from -0.046875 to 0.046875
- gate_a: bfloat16 [4096, 64], P('tensor'), may hold values from -0.09375 to 0.09375
- gate_b: bfloat16 [64, 18432], P(None, 'tensor'), may hold values from -0.75 to 0.75
- up_a: bfloat16 [4096, 64], P('tensor'), may hold values from -0.09375 to 0.09375
- up_b: bfloat16 [64, 18432], P(None, 'tensor'), may hold values from -0.75 to 0.75
- down_a: bfloat16 [18432, 64], P('tensor'), may hold values from -0.046875 to 0.046875
- down_adapter_second: bfloat16 [64, 4096], P(None, 'tensor'), may hold values from -0.75 to 0.75
Outputs:
- gate_first_gradient: float32 [4096, 64], P('tensor')
- gate_second_gradient: float32 [64, 18432], P(None, 'tensor')
- up_first_gradient: float32 [4096, 64], P('tensor')
- up_second_gradient: float32 [64, 18432], P(None, 'tensor')
- grad_down_a: float32 [18432, 64], P('tensor')
- down_second_gradient: float32 [64, 4096], P(None, 'tensor')
All inputs are finite; a program needn't handle non-finite values.
Results may differ from a plain program's by a relative error of at most 0.005.
Values may be sent and summed in bfloat16 or wider, within the bound.
A program may use at most 64 MiB of HBM per device.

v0:
```python
import jax
import jax.numpy as jnp
from jax import lax
from jax.sharding import PartitionSpec as P

adapter_scale_factor = 2.0


def silu_parts(pre):
    sigma = jax.nn.sigmoid(pre)
    return (pre * sigma, sigma * (1.0 + pre * (1.0 - sigma)))


def matrix_multiply(left, right):
    return jnp.dot(left, right, preferred_element_type=jnp.float32)


def contract_last(left, right):
    return lax.dot_general(
        left, right, (((1,), (1,)), ((), ())), preferred_element_type=jnp.float32
    )


def contract_leading_axis(left, right):
    return lax.dot_general(
        left, right, (((0,), (0,)), ((), ())), preferred_element_type=jnp.float32
    )


def local(
    inputs,
    cotangent,
    gate_pre,
    up_pre,
    down_weight,
    gate_a,
    gate_b,
    up_a,
    up_b,
    down_a,
    down_adapter_second,
):
    gate_wide = gate_pre.astype(jnp.float32)
    up_wide = up_pre.astype(jnp.float32)
    active, slope = silu_parts(gate_wide)
    hidden = (active * up_wide).astype(jnp.bfloat16)
    gate_part = matrix_multiply(inputs, gate_a)
    up_part = matrix_multiply(inputs, up_a)
    down_part = matrix_multiply(hidden, down_a)
    back_part = contract_last(cotangent, down_adapter_second)
    gate_sum, up_sum, down_sum, backward_total_sum = lax.psum(
        (gate_part, up_part, down_part, back_part), "tensor"
    )
    hidden_base = contract_last(
        lax.all_gather(cotangent, "tensor", axis=1, tiled=True), down_weight
    )
    gate_reduced_rank = gate_sum.astype(jnp.bfloat16)
    up_reduced_rank = up_sum.astype(jnp.bfloat16)
    down_reduced_rank = down_sum.astype(jnp.bfloat16)
    down_backward = (adapter_scale_factor * backward_total_sum).astype(jnp.bfloat16)
    hidden_grad = hidden_base + contract_last(down_backward, down_a)
    grad_down_a = contract_leading_axis(hidden, down_backward)
    down_second_gradient = adapter_scale_factor * contract_leading_axis(
        down_reduced_rank, cotangent
    )
    gate_gradient = (hidden_grad * up_wide * slope).astype(jnp.bfloat16)
    up_gradient = (hidden_grad * active).astype(jnp.bfloat16)
    gate_total, up_total = lax.psum(
        (contract_last(gate_gradient, gate_b), contract_last(up_gradient, up_b)), "tensor"
    )
    gate_backward = gate_total.astype(jnp.bfloat16)
    up_backward = up_total.astype(jnp.bfloat16)
    gate_second_gradient = adapter_scale_factor * contract_leading_axis(
        gate_reduced_rank, gate_gradient
    )
    up_second_gradient = adapter_scale_factor * contract_leading_axis(up_reduced_rank, up_gradient)
    gate_first_gradient = adapter_scale_factor * contract_leading_axis(inputs, gate_backward)
    up_first_gradient = adapter_scale_factor * contract_leading_axis(inputs, up_backward)
    (
        gate_first_gradient,
        gate_second_gradient,
        up_first_gradient,
        up_second_gradient,
        grad_down_a,
        down_second_gradient,
    ) = lax.psum(
        (
            gate_first_gradient,
            gate_second_gradient,
            up_first_gradient,
            up_second_gradient,
            grad_down_a,
            down_second_gradient,
        ),
        "dp",
    )
    return (
        gate_first_gradient,
        gate_second_gradient,
        up_first_gradient,
        up_second_gradient,
        grad_down_a,
        down_second_gradient,
    )


def solution(mesh):
    placed = (
        P("dp", "tensor"),
        P("dp", "tensor"),
        P("dp", "tensor"),
        P("dp", "tensor"),
        P("tensor", None),
        P("tensor", None),
        P(None, "tensor"),
        P("tensor", None),
        P(None, "tensor"),
        P("tensor", None),
        P(None, "tensor"),
    )
    return jax.shard_map(
        local,
        mesh=mesh,
        in_specs=placed,
        out_specs=(
            P("tensor", None),
            P(None, "tensor"),
            P("tensor", None),
            P(None, "tensor"),
            P("tensor", None),
            P(None, "tensor"),
        ),
        check_vma=False,
    )
```

profile of v0, /device:TPU:1, one launch (start us, length us, event | category | flops | bytes accessed | tf_op | source)
XLA Modules:
  0.0 366.5 jit_solution(13864340921963029003)
XLA Ops:
  7.2 0.0 copy-start
  7.2 0.0 all-gather.2.cloned.1.call-start
  7.2 0.7 all-gather.2.cloned.1.call-update
  7.9 0.0 all-reduce.6.cloned.1.call-start
  8.0 1.9 fusion.19
  9.9 0.0 all-reduce.6.cloned.1.call-update
  9.9 0.0 all-reduce.8.cloned.1.call-start
  10.0 0.0 copy-done
  10.0 1.8 fusion.21
  11.7 1.8 fusion.23
  13.5 0.0 copy-start.9
  13.5 56.9 %all-gather.2.cloned.1.call-done = bf16[768,4096]{1,0:T(8,128)(2,1)} async-done(((bf16[768,256]{1,0:T(8,128)(2,1)}), bf16[768,4096]{1,0:T(8,128)(2,1)}) %all-gather.2.cloned.1.call-update) | async-done | bytes 6291472 | tf_op jit(solution)/shard_map/all_gather | solution.py:55
  70.4 13.7 %fusion.18 = f32[768,1152]{1,0:T(8,128)} fusion(bf16[768,4096]{1,0:T(8,128)(2,1)} %all-gather.2.cloned.1.call-done, bf16[1152,4096]{1,0:T(8,128)(2,1)} %param.15), kind=kOutput, calls=%fused_computation.31 | convolution fusion | flops 7247757312 | bytes 19267584 | tf_op jit(solution)/shard_map/dot_general | solution.py:19
  84.1 0.0 copy-start.7
  84.1 0.0 copy-start.8
  84.1 91.9 %all-reduce.6.cloned.1.call-done = f32[768,64]{0,1:T(8,128)} async-done(((f32[768,64]{0,1:T(8,128)}), f32[768,64]{0,1:T(8,128)}) %all-reduce.6.cloned.1.call-update) | async-done | bytes 196624 | tf_op jit(solution)/shard_map/psum | solution.py:51
  176.0 0.0 copy-done.9
  176.0 5.4 %multiply_convert_fusion = (bf16[768,1152]{1,0:T(8,128)(2,1)S(1)}, bf16[768,1152]{1,0:T(8,128)(2,1)S(1)}, bf16[768,1152]{1,0:T(8,128)(2,1)S(1)}) fusion(bf16[768,1152]{1,0:T(8,128)(2,1)} %param.13, bf16[768,1152]{1,0:T(8,128)(2,1)} %param.14, f32[768,1152]{1,0:T(8,128)} %fusion.18, bf16[1152,64]{0,1:T(8,128)(2,1)S(1)} %copy-done.9, ...), kind=kOutput, calls=%fused_computation.14 | convolution fusion | flops 129269760 | bytes 12730368 | tf_op jit(solution)/shard_map/dot_general | solution.py:19
  181.4 0.0 copy-start.1
  181.4 0.0 copy-start.3
  181.4 0.0 copy-done.7
  181.5 0.6 fusion.20
  182.1 0.6 copy-done.1
  182.7 0.0 copy-done.8
  182.7 0.6 fusion.22
  183.3 0.0 copy-done.3
  183.3 1.4 fusion.24
  184.7 0.0 copy-start.4
  184.7 57.3 %all-reduce.9 = (bf16[768,64]{1,0:T(8,128)(2,1)}, bf16[768,64]{1,0:T(8,128)(2,1)}, bf16[768,64]{1,0:T(8,128)(2,1)}, bf16[768,64]{1,0:T(8,128)(2,1)S(1)}, bf16[768,64]{1,0:T(8,128)(2,1)}) all-reduce(f32[768,64]{1,0:T(8,128)S(1)} %fusion.20, f32[768,64]{1,0:T(8,128)} %fusion.21, ...), channel_id=1, replica_groups=mesh['dp'=16,'tensor'=16] {'tensor'}, use_global_device_ids=true, to_apply=%region_1.0 | all-reduce | flops 245760 | bytes 1474560 | tf_op jit(solution)/shard_map/psum | solution.py:68
  241.9 0.0 copy-start.2
  241.9 0.0 copy-start.6
  241.9 0.0 copy-start.5
  241.9 1.9 fusion.9
  243.9 2.7 convolution_multiply_fusion.1
  246.6 1.8 fusion.8
  248.4 0.0 copy-done.2
  248.4 1.1 convolution_multiply_fusion
  249.6 0.0 copy-done.4
  249.6 0.0 copy-done.6
  249.6 0.9 convolution_multiply_fusion.2
  250.5 0.0 copy-done.5
  250.5 1.1 fusion.15
  251.6 0.0 all-reduce.8.cloned.1.call-update
  251.6 98.8 %all-reduce.8.cloned.1.call-done = (f32[256,64]{0,1:T(8,128)}, f32[64,1152]{1,0:T(8,128)}, f32[256,64]{0,1:T(8,128)}, f32[64,1152]{1,0:T(8,128)}, f32[1152,64]{0,1:T(8,128)}, /*index=5*/f32[64,256]{1,0:T(8,128)}) async-done(((f32[256,64]{0,1:T(8,128)}, f32[64,1152]{1,0:T(8,128)}, f32[256,64]{0,1:T(8,128)}, f32[64,1152]{1,0:T(8,128)}, f32[1152,64]{0,1:T(8,128)}, /*index=5*/f32[64,256]{1,0:T(8,128)}), ...) | async-done | bytes 1081360 | tf_op jit(solution)/shard_map/psum | solution.py:86
  350.5 1.5 copy.34
  351.9 1.7 copy.35
  353.6 1.5 copy.36
  355.1 1.7 copy.37
  356.8 1.7 copy.38
  358.5 1.5 copy.39
Async XLA Ops:
  7.2 2.8 copy-start
  7.2 63.3 %all-gather.2.cloned.1.call-start = ((), (), s32[]{:S(2)}) async-start(), calls=%async_computation | async-start | bytes 6684672 | tf_op jit(solution)/shard_map/all_gather | solution.py:55
  7.9 168.1 %all-reduce.6.cloned.1.call-start = ((), (), s32[]{:S(2)}) async-start(), calls=%async_computation.1 | async-start | bytes 393216 | tf_op jit(solution)/shard_map/psum | solution.py:51
  9.9 340.5 %all-reduce.8.cloned.1.call-start = ((), (), s32[]{:S(2)}) async-start(), calls=%async_computation.2 | async-start | bytes 2162688 | tf_op jit(solution)/shard_map/psum | solution.py:86
  13.5 162.5 %copy-start.9 = (bf16[1152,64]{0,1:T(8,128)(2,1)S(1)}, bf16[1152,64]{0,1:T(8,128)(2,1)}, u32[]{:S(2)}) copy-start(bf16[1152,64]{0,1:T(8,128)(2,1)} %param.20) | copy-start | bytes 442372
  84.1 97.3 %copy-start.7 = (bf16[64,1152]{1,0:T(8,128)(2,1)S(1)}, bf16[64,1152]{1,0:T(8,128)(2,1)}, u32[]{:S(2)}) copy-start(bf16[64,1152]{1,0:T(8,128)(2,1)} %param.17) | copy-start | bytes 442372
  84.1 98.6 %copy-start.8 = (bf16[64,1152]{1,0:T(8,128)(2,1)S(1)}, bf16[64,1152]{1,0:T(8,128)(2,1)}, u32[]{:S(2)}) copy-start(bf16[64,1152]{1,0:T(8,128)(2,1)} %param.19) | copy-start | bytes 442372
  181.4 1.2 copy-start.1
  181.4 1.9 copy-start.3
  184.7 64.9 %copy-start.4 = (bf16[768,256]{1,0:T(8,128)(2,1)S(1)}, bf16[768,256]{1,0:T(8,128)(2,1)}, u32[]{:S(2)}) copy-start(bf16[768,256]{1,0:T(8,128)(2,1)} %param.12) | copy-start | bytes 1179652
  241.9 6.5 %copy-start.2 = (bf16[768,1152]{1,0:T(8,128)(2,1)S(1)}, bf16[768,1152]{1,0:T(8,128)(2,1)}, u32[]{:S(2)}) copy-start(bf16[768,1152]{1,0:T(8,128)(2,1)} %copy-done.1) | copy-start | bytes 5308420
  241.9 7.6 %copy-start.6 = (bf16[768,64]{1,0:T(8,128)(2,1)S(1)}, bf16[768,64]{1,0:T(8,128)(2,1)}, u32[]{:S(2)}) copy-start(bf16[768,64]{1,0:T(8,128)(2,1)} %get-tuple-element.10) | copy-start | bytes 294916
  241.9 8.5 %copy-start.5 = (f32[768,64]{0,1:T(8,128)S(1)}, f32[768,64]{0,1:T(8,128)}, u32[]{:S(2)}) copy-start(f32[768,64]{0,1:T(8,128)} %all-reduce.6.cloned.1.call-done) | copy-start | bytes 589828
Sparse Core Ops, SparseCore 0:
  9.8 60.6 all-gather.1
  73.3 102.6 all-reduce.5
  251.7 98.6 all-reduce.7
where the time goes:
time: 368 us; the launch traced here: 366 us
  waiting for transfers between devices  248 us (67%)
  blocking collectives  57.3 us (16%)
  matrix products  36.8 us (10%)
  between operations  13.8 us (4%)
  local copies, waits for them, and re-layouts  10.1 us (3%)
    psum x1, waiting for transfers between devices, local(): lax.psum((gate_first_gradient, gate_second_gradient, up_first_gradient, u...  98.8 us
    psum x1, waiting for transfers between devices, local(): lax.psum((gate_part, up_part, down_part, back_part), 'tensor')  91.9 us
    psum x1, blocking collectives, local(): lax.psum((contract_last(gate_gradient, gate_b), contract_last(up_gradient...  57.3 us
    all_gather x1, waiting for transfers between devices, local(): lax.all_gather(cotangent, 'tensor', axis=1, tiled=True)  56.9 us
    dot_general x5, matrix products, contract_last(): lax.dot_general(left, right, (((1,), (1,)), ((), ())), preferred_element_...  22.2 us
    unnamed x26, local copies, waits for them, and re-layouts  10.1 us
    dot_general x6, matrix products, contract_leading_axis(): lax.dot_general(left, right, (((0,), (0,)), ((), ())), preferred_element_...  9.64 us
  transfers between devices with their start and end apart: 3, of which 3 were waited for; matrix products, arithmetic and copies ran while one was open for 5% of the time, Pallas kernels for 0%

commit v1 on v0

v1 whole, which is shorter than its diff:
```python
import functools

import jax
import jax.numpy as jnp
from jax import lax
from jax.experimental import pallas as pl
from jax.experimental.pallas import tpu as pltpu
from jax.sharding import PartitionSpec as P

MESH = pl.DeviceIdType.MESH
F32, BF16 = jnp.float32, jnp.bfloat16
CHUNKS = 4
SCALE = 2.0


def dot_nn(a, b):
    return jnp.dot(a, b, preferred_element_type=F32)


def dot_nt(a, b):
    return lax.dot_general(a, b, (((1,), (1,)), ((), ())), preferred_element_type=F32)


def pick(i, values):
    out = values[0]
    for k in range(1, len(values)):
        out = jnp.where(i == k, values[k], out)
    return out


def arrival_order(hops, chunks, ahead=3):
    events, sent, own = [], [], 0

    def run(event):
        events.append(event)
        if event[0] < hops:
            sent.append((event[0] + 1, event[1]))

    while own < min(ahead, chunks):
        run((0, own))
        own += 1
    at = 0
    while at < len(sent):
        run(sent[at])
        at += 1
        if at % 2 == 0 and own < chunks:
            run((0, own))
            own += 1
    return events


def main_kernel(
    nz, nd,
    x_hbm, c_hbm, g_hbm, u_hbm, w_hbm, ga_hbm, gb_hbm, ua_hbm, ub_hbm, da_hbm, ds_hbm,
    oa_hbm, ob_hbm, oc_hbm,
    cg, wv, gv, uv, act, usl, hid, xin, wf, wd, acc,
    lp, lpr, lsb, lrb, low, lowt,
    bp, bpr, bsb, brb, bk,
    gs, us, gda, dsec, gg, ug,
    sa, ra, ta, sb, rb, tb, sc, rc, tc,
    in_sem, w_sem, ring_recv, pair_recv, ring_send, pair_send, red_sem, dp_sem, out_sem,
):
    tokens, d_local = x_hbm.shape
    f_local = g_hbm.shape[1]
    rank = gb_hbm.shape[0]
    nt = 2 * nz
    hops = nz // 2
    rows = tokens // CHUNKS
    half = tokens // 2
    part = half // nz
    group = 16 // nd

    t_me = lax.axis_index("tensor")
    d_me = lax.axis_index("dp")
    z = t_me // 2
    c = t_me % 2
    way = 1 - 2 * c

    def at_z(offset):
        return lax.rem(z + offset + 2 * nz, nz)

    def block(offset, core):
        return 2 * at_z(offset) + core

    def remote(src, dst, send, recv, **where):
        return pltpu.make_async_remote_copy(
            src_ref=src, dst_ref=dst, send_sem=send, recv_sem=recv, device_id=where, device_id_type=MESH)

    def wait_bytes(ref, sem):
        pltpu.make_async_copy(ref, ref, sem).wait()

    loads = [
        pltpu.make_async_copy(c_hbm, cg.at[t_me], in_sem.at[0]),
        pltpu.make_async_copy(g_hbm, gv, in_sem.at[1]),
        pltpu.make_async_copy(u_hbm, uv, in_sem.at[2]),
        pltpu.make_async_copy(x_hbm, xin, in_sem.at[3]),
        pltpu.make_async_copy(ga_hbm, wd.at[0:rank], in_sem.at[4]),
        pltpu.make_async_copy(ua_hbm, wd.at[rank:2 * rank], in_sem.at[5]),
        pltpu.make_async_copy(ds_hbm, wd.at[3 * rank:4 * rank], in_sem.at[6]),
        pltpu.make_async_copy(gb_hbm, wf.at[0:rank], in_sem.at[7]),
        pltpu.make_async_copy(ub_hbm, wf.at[2 * rank:3 * rank], in_sem.at[8]),
        pltpu.make_async_copy(da_hbm, wf.at[4 * rank:5 * rank], in_sem.at[9]),
    ]
    for copy in loads:
        copy.start()
    w_loads = [
        pltpu.make_async_copy(w_hbm.at[:, k * d_local:(k + 1) * d_local], wv.at[k], w_sem) for k in range(nt)
    ]
    for copy in w_loads:
        copy.start()

    barrier = pltpu.get_barrier_semaphore()
    for k in range(1, nz):
        pl.semaphore_signal(barrier, inc=1, device_id={"tensor": block(k, c)}, device_id_type=MESH)
    pl.semaphore_signal(barrier, inc=1, device_id={"tensor": 2 * z + 1 - c}, device_id_type=MESH)
    for k in range(1, nd):
        pl.semaphore_signal(barrier, inc=1, device_id={"dp": lax.rem(d_me + k, nd)}, device_id_type=MESH)

    zeros = jnp.zeros((rank, f_local), BF16)
    wf[rank:2 * rank] = zeros
    wf[3 * rank:4 * rank] = zeros
    wf[5 * rank:6 * rank] = zeros
    wd[2 * rank:3 * rank] = jnp.zeros((rank, d_local), BF16)
    for r in range(4):
        sa[4 * r + 3, :, d_local:] = jnp.zeros((16, sa.shape[2] - d_local), BF16)
        for k in (1, 3):
            sb[4 * r + k, :, f_local - 640:] = jnp.zeros((16, 1280 - f_local), BF16)
    gs[...] = jnp.zeros_like(gs)
    us[...] = jnp.zeros_like(us)

    loads[0].wait()
    pl.semaphore_wait(barrier, nz + nd - 1)

    def piece(owner, core, q):
        return cg.at[block(owner, core), q * rows:(q + 1) * rows]

    def ring_slot(hop, down):
        return 2 * (hop - 1) + down

    def arrivals(hop):
        if hop == hops:
            return [(2 * (hops - 1), hops)]
        return [(ring_slot(hop, 0), -hop), (ring_slot(hop, 1), hop)]

    def pass_on(hop, q):
        if hop + 1 < hops:
            for down, step in ((0, 1), (1, -1)):
                src = piece(-step * hop, c, q)
                remote(src, src, ring_send, ring_recv.at[ring_slot(hop + 1, down), q],
                       tensor=block(step, c)).start()
        elif hop + 1 == hops:
            src = piece(-way * hop, c, q)
            remote(src, src, ring_send, ring_recv.at[2 * (hops - 1), q], tensor=block(way, c)).start()
        slots = [(0, 0)] if hop == 0 else [(s + 1, o) for s, o in arrivals(hop)]
        for slot, offset in slots:
            src = piece(offset, c, q)
            remote(src, src, pair_send, pair_recv.at[slot, q], tensor=2 * z + 1 - c).start()
        return [(slot, offset, q) for slot, offset in slots]

    def multiply(items):
        if not items:
            return
        blocks = [b for b, _ in items]
        qs = [q for _, q in items]

        def body(i, carry):
            b, q = pick(i, blocks), pick(i, qs)
            at = pl.multiple_of(q * rows, 16)
            acc[q] += dot_nt(cg[b, pl.ds(at, rows)], wv[b])
            return carry

        lax.fori_loop(0, len(items), body, 0)

    def prepare(q):
        def body(i, carry):
            at = pl.multiple_of(q * rows + i * 16, 16)
            g = gv[pl.ds(at, 16)].astype(F32)
            u = uv[pl.ds(at, 16)].astype(F32)
            s = 0.5 * jnp.tanh(0.5 * g) + 0.5
            a = g * s
            inner = pl.multiple_of(i * 16, 16)
            act[q, pl.ds(inner, 16)] = a
            usl[q, pl.ds(inner, 16)] = u * (s * (1.0 + (g - a)))
            hid[pl.ds(at, 16)] = (a * u).astype(BF16)
            return carry

        lax.fori_loop(0, rows // 16, body, 0)
        acc[q] = jnp.zeros((rows, f_local), F32)
        here = slice(q * rows, (q + 1) * rows)
        lp[here, :2 * rank] = dot_nt(xin[here], wd[:2 * rank])
        own = cg[t_me, q * rows:(q + 1) * rows]
        lp[here, 2 * rank:] = dot_nt(hid[here], wf[4 * rank:6 * rank]) + SCALE * dot_nt(own, wd[2 * rank:4 * rank])

    def z_steps(full, recv, out_b, in_b, result, base):
        mine = pl.ds(pl.multiple_of(c * half, 16), half)
        other = pl.ds(pl.multiple_of((1 - c) * half, 16), half)
        slice_rows = pl.ds(pl.multiple_of(c * half + z * part, 16), part)

        def exchange():
            remote(full.at[other], recv, red_sem.at[base], red_sem.at[base + 1], tensor=2 * z + 1 - c).start()

        def scatter():
            wait_bytes(recv, red_sem.at[base + 1])
            recv[...] += full[mine]
            for k in range(nz):
                out_b[k] = recv[k * part:(k + 1) * part].astype(BF16)
            for k in range(1, nz):
                to = at_z(k)
                remote(out_b.at[to], in_b.at[k - 1], red_sem.at[base + 2], red_sem.at[base + 3],
                       tensor=2 * to + c).start()

        def gather():
            wait_bytes(in_b, red_sem.at[base + 3])
            total = recv[pl.ds(pl.multiple_of(z * part, 16), part)]
            for k in range(nz - 1):
                total += in_b[k].astype(F32)
            result[slice_rows] = total.astype(BF16)
            for k in range(1, nz):
                remote(result.at[slice_rows], result.at[slice_rows], red_sem.at[base + 4], red_sem.at[base + 5],
                       tensor=block(k, c)).start()

        def share():
            wait_bytes(result.at[0:(nz - 1) * part], red_sem.at[base + 5])
            remote(result.at[mine], result.at[mine], red_sem.at[base + 6], red_sem.at[base + 7],
                   tensor=2 * z + 1 - c).start()

        def finish():
            wait_bytes(result.at[0:half], red_sem.at[base + 7])

        def drain():
            wait_bytes(recv, red_sem.at[base])
            wait_bytes(in_b, red_sem.at[base + 2])
            wait_bytes(result.at[0:(nz - 1) * part], red_sem.at[base + 4])
            wait_bytes(result.at[0:half], red_sem.at[base + 6])

        return exchange, scatter, gather, share, finish, drain

    def dp_steps(out_b, in_b, total_b, result, base):
        def scatter():
            for k in range(1, nd):
                to = lax.rem(d_me + k, nd)
                remote(out_b.at[pl.ds(to * group, group)], in_b.at[k - 1], dp_sem.at[base], dp_sem.at[base + 1],
                       dp=to).start()

        def gather():
            wait_bytes(in_b, dp_sem.at[base + 1])
            total = out_b[pl.ds(d_me * group, group)].astype(F32)
            for k in range(nd - 1):
                total += in_b[k].astype(F32)
            total_b[...] = total.astype(BF16)
            place = result.at[pl.ds(d_me * group, group)]
            for k in range(1, nd):
                remote(total_b, place, dp_sem.at[base + 2], dp_sem.at[base + 3], dp=lax.rem(d_me + k, nd)).start()
            pltpu.make_async_copy(total_b, place, out_sem.at[base // 4]).start()

        def finish():
            place = result.at[pl.ds(d_me * group, group)]
            pltpu.make_async_copy(total_b, place, out_sem.at[base // 4]).wait()
            wait_bytes(result.at[0:(nd - 1) * group], dp_sem.at[base + 3])
            wait_bytes(in_b, dp_sem.at[base])
            wait_bytes(result.at[0:(nd - 1) * group], dp_sem.at[base + 2])

        return scatter, gather, finish

    lows = z_steps(lp, lpr, lsb, lrb, low, 0)
    backs = z_steps(bp, bpr, bsb, brb, bk, 8)
    first_dp = dp_steps(sa, ra, ta, oa_hbm, 0)
    second_dp = dp_steps(sb, rb, tb, ob_hbm, 4)
    third_dp = dp_steps(sc, rc, tc, oc_hbm, 8)

    def use_lows():
        lows[4]()
        for q in range(CHUNKS):
            lowt[q] = jnp.transpose(low[q * rows:(q + 1) * rows].astype(F32)).astype(BF16)
        gda[...] = jnp.zeros_like(gda)
        dsec[...] = jnp.zeros_like(dsec)

        def body(q, carry):
            at = pl.ds(pl.multiple_of(q * rows, 16), rows)
            gda[...] += dot_nn(lowt[q, 3 * rank:], hid[at])
            dsec[...] += dot_nn(lowt[q, 2 * rank:3 * rank], cg[t_me, at])
            return carry

        lax.fori_loop(0, CHUNKS, body, 0)
        third = f_local // 3
        for r in range(4):
            at = slice(16 * r, 16 * r + 16)
            for k in range(3):
                sa[4 * r + k] = gda[at, k * third:(k + 1) * third].astype(BF16)
            sa[4 * r + 3, :, :d_local] = (SCALE * dsec[at]).astype(BF16)
        first_dp[0]()

    def post(q):
        lowq = low[q * rows:(q + 1) * rows, 2 * rank:]
        width = f_local // 3

        def body(i, carry):
            cols = pl.ds(pl.multiple_of(i * width, 128), width)
            grad = acc[q, :, cols] + dot_nn(lowq, wf[3 * rank:5 * rank, cols])
            gg[:, cols] = (grad * usl[q, :, cols]).astype(BF16)
            ug[:, cols] = (grad * act[q, :, cols]).astype(BF16)
            return carry

        lax.fori_loop(0, 3, body, 0)
        bp[q * rows:(q + 1) * rows] = dot_nt(gg[...], wf[:2 * rank]) + dot_nt(ug[...], wf[rank:3 * rank])
        gs[...] += dot_nn(lowt[q, :rank], gg[...])
        us[...] += dot_nn(lowt[q, rank:2 * rank], ug[...])

    events = arrival_order(hops, CHUNKS)
    left = {q: 2 * nz for q in range(CHUNKS)}
    waiting, todo, seen, done = [], [], 0, []
    plan = {
        0: [lambda: prepare(2)],
        1: [lambda: prepare(3), lows[0]],
        3: [lows[1]],
        5: [lows[2]],
        7: [lows[3]],
        8: [use_lows],
        11: [first_dp[1]],
    }
    last_step = 8 * (CHUNKS * hops) // 16
    scale = lambda k: k * (CHUNKS * hops) // 16
    steps = {}
    for k, fs in plan.items():
        steps.setdefault(scale(k), []).extend(fs)
    posted = 0
    ready = False

    def settle():
        found = []
        for slot, offset, q in waiting:
            wait_bytes(piece(offset, 1 - c, q), pair_recv.at[slot, q])
            found.append((block(offset, 1 - c), q))
        waiting.clear()
        return found

    started = False
    for hop, q in events:
        if hop == 0:
            fresh = pass_on(0, q)
            todo.append((t_me, q))
            waiting.extend(fresh)
            continue
        if not started:
            for copy in loads[1:]:
                copy.wait()
            prepare(0)
            prepare(1)
            wait_bytes(wv, w_sem)
            started = True
        items = [(block(offset, c), q) for _, offset in arrivals(hop)]
        for slot, offset in arrivals(hop):
            wait_bytes(piece(offset, c, q), ring_recv.at[slot, q])
        fresh = pass_on(hop, q)
        items = settle() + items + todo
        todo.clear()
        for f in steps.get(seen, []):
            f()
        held = [(b, p) for b, p in items if p >= 2 + seen]
        items = [(b, p) for b, p in items if p < 2 + seen]
        todo.extend(held)
        multiply(items)
        for _, p in items:
            left[p] -= 1
        waiting.extend(fresh)
        seen += 1
        while posted < CHUNKS and left[posted] == 0:
            post(posted)
            posted += 1
    items = settle() + todo
    multiply(items)
    while posted < CHUNKS:
        post(posted)
        posted += 1

    backs[0]()
    for r in range(4):
        at = slice(16 * r, 16 * r + 16)
        for k, full in ((0, gs), (2, us)):
            sb[4 * r + k] = (SCALE * full[at, :640]).astype(BF16)
            sb[4 * r + k + 1, :, :f_local - 640] = (SCALE * full[at, 640:]).astype(BF16)
    second_dp[0]()
    backs[1]()
    backs[2]()
    second_dp[1]()
    backs[3]()
    backs[4]()
    back_t = jnp.transpose(bk[...].astype(F32)).astype(BF16)
    firsts = SCALE * dot_nn(back_t, xin[...])
    for r in range(4):
        for k in range(2):
            for m in range(2):
                sc[4 * r + 2 * k + m] = firsts[
                    k * rank + 16 * r:k * rank + 16 * r + 16, 128 * m:128 * m + 128].astype(BF16)
    third_dp[0]()
    third_dp[1]()
    lows[5]()
    backs[5]()
    wait_bytes(cg.at[0:2 * hops - 1], ring_send)
    wait_bytes(cg.at[0:2 * hops], pair_send)
    first_dp[2]()
    second_dp[2]()
    third_dp[2]()


def unpack_kernel(a_ref, b_ref, c_ref, gf, gs, uf, us, gda, dsec):
    f_local = gs.shape[1]
    d_local = gf.shape[1]
    third = f_local // 3
    for r in range(4):
        at = slice(16 * r, 16 * r + 16)
        for k in range(3):
            gda[at, k * third:(k + 1) * third] = a_ref[4 * r + k].astype(F32)
        dsec[at] = a_ref[4 * r + 3, :, :d_local].astype(F32)
        for k, full in ((0, gs), (2, us)):
            full[at, :640] = b_ref[4 * r + k].astype(F32)
            full[at, 640:] = b_ref[4 * r + k + 1, :, :f_local - 640].astype(F32)
        for k, full in ((0, gf), (2, uf)):
            full[at, :128] = c_ref[4 * r + k].astype(F32)
            full[at, 128:] = c_ref[4 * r + k + 1].astype(F32)


def local(nz, nd, inputs, cotangent, gate_pre, up_pre, down_weight, gate_a, gate_b, up_a, up_b, down_a, down_second):
    tokens, d_local = inputs.shape
    f_local = gate_pre.shape[1]
    rank = gate_b.shape[0]
    nt, hops = 2 * nz, nz // 2
    rows, half = tokens // CHUNKS, tokens // 2
    part, group = half // nz, 16 // nd
    wide_a, wide_b, wide_c = f_local // 3, 640, 128
    any_space = pl.BlockSpec(memory_space=pl.ANY)
    vmem, dma = pltpu.VMEM, pltpu.SemaphoreType.DMA

    def dp_buffers(width):
        return [vmem((16, 16, width), BF16), vmem((nd - 1, group, 16, width), BF16), vmem((group, 16, width), BF16)]

    def z_buffers(width):
        return [vmem((tokens, width), F32), vmem((half, width), F32), vmem((nz, part, width), BF16),
                vmem((nz - 1, part, width), BF16), vmem((tokens, width), BF16)]

    scratch = [
        vmem((nt, tokens, d_local), BF16),
        vmem((nt, f_local, d_local), BF16),
        vmem((tokens, f_local), BF16),
        vmem((tokens, f_local), BF16),
        vmem((CHUNKS, rows, f_local), F32),
        vmem((CHUNKS, rows, f_local), F32),
        vmem((tokens, f_local), BF16),
        vmem((tokens, d_local), BF16),
        vmem((6 * rank, f_local), BF16),
        vmem((4 * rank, d_local), BF16),
        vmem((CHUNKS, rows, f_local), F32),
        *z_buffers(4 * rank),
        vmem((CHUNKS, 4 * rank, rows), BF16),
        *z_buffers(2 * rank),
        vmem((rank, f_local), F32),
        vmem((rank, f_local), F32),
        vmem((rank, f_local), F32),
        vmem((rank, d_local), F32),
        vmem((rows, f_local), BF16),
        vmem((rows, f_local), BF16),
        *dp_buffers(wide_a),
        *dp_buffers(wide_b),
        *dp_buffers(wide_c),
        dma((10,)),
        dma,
        dma((2 * hops - 1, CHUNKS)),
        dma((2 * hops, CHUNKS)),
        dma,
        dma,
        dma((16,)),
        dma((12,)),
        dma((3,)),
    ]
    packed = pl.pallas_call(
        functools.partial(main_kernel, nz, nd),
        out_shape=[jax.ShapeDtypeStruct((16, 16, w), BF16) for w in (wide_a, wide_b, wide_c)],
        in_specs=[any_space] * 11,
        out_specs=[any_space] * 3,
        scratch_shapes=scratch,
        compiler_params=pltpu.CompilerParams(
            collective_id=0, has_side_effects=True, vmem_limit_bytes=56 * 1024 * 1024),
        name="adapters",
    )(inputs, cotangent, gate_pre, up_pre, down_weight, gate_a.T, gate_b, up_a.T, up_b, down_a.T, down_second)
    small = jax.ShapeDtypeStruct((rank, d_local), F32)
    large = jax.ShapeDtypeStruct((rank, f_local), F32)
    gf, gs, uf, us, gda, dsec = pl.pallas_call(
        unpack_kernel, out_shape=[small, large, small, large, large, small], name="unpack")(*packed)
    return gf.T, gs, uf.T, us, gda.T, dsec


def solution(mesh):
    split, rows, columns = P("dp", "tensor"), P("tensor", None), P(None, "tensor")
    return jax.shard_map(
        functools.partial(local, mesh.shape["tensor"] // 2, mesh.shape["dp"]),
        mesh=mesh,
        in_specs=(split, split, split, split, rows, rows, columns, rows, columns, rows, columns),
        out_specs=(rows, columns, rows, columns, rows, columns),
        check_vma=False,
    )
```

time: 368 us -> 86.6 us (0.24)
  waiting for transfers between devices: 248 us -> 0 us
  Pallas kernels: 0 us -> 85.9 us
  blocking collectives: 57.3 us -> 0 us
  matrix products: 36.8 us -> 0 us
  between operations: 13.8 us -> 0.64 us
  local copies, waits for them, and re-layouts: 10.1 us -> 0 us
    psum x2 -> x0, waiting for transfers between devices: 191 us -> none  [the longest x1 98.8 us: local(): lax.psum((gate_first_gradient, gate_second_gradient, up_first_gradient, u...]
    pallas_call x0 -> x2, Pallas kernels: none -> 85.9 us  [the longest x1 83.9 us: local(): pl.pallas_call(functools.partial(main_kernel, nz, nd), out_shape=[jax.Sha...]
    psum x1 -> x0, blocking collectives: 57.3 us -> none  [local(): lax.psum((contract_last(gate_gradient, gate_b), contract_last(up_gradient...]
    all_gather x1 -> x0, waiting for transfers between devices: 56.9 us -> none  [local(): lax.all_gather(cotangent, 'tensor', axis=1, tiled=True)]
    dot_general x14 -> x0, matrix products: 36.8 us -> none  [the longest x5 22.2 us: contract_last(): lax.dot_general(left, right, (((1,), (1,)), ((), ())), preferred_element_...]
    unnamed x26 -> x0, local copies, waits for them, and re-layouts: 10.1 us -> none
  transfers between devices with their start and end apart: 3 -> 0, of which waited for: 3 -> 0; matrix products, arithmetic and copies ran while one was open for 5% -> 0% of each run, Pallas kernels for 0% -> 0%
where the time goes in v1:
time: 86.6 us; the launch traced here: 86.5 us
  Pallas kernels  85.9 us (99%)
    pallas_call x1, Pallas kernels, local(): pl.pallas_call(functools.partial(main_kernel, nz, nd), out_shape=[jax.Sha...  83.9 us
    pallas_call x1, Pallas kernels, local(): pl.pallas_call(unpack_kernel, out_shape=[small, large, small, large, larg...  2.04 us

profile of v1, /device:TPU:1, one launch (start us, length us, event | category | flops | bytes accessed | tf_op | source)
XLA Modules:
  0.0 86.5 jit_solution(4264057371570836897)
XLA Ops:
  0.6 83.9 %adapters.1 = (bf16[16,16,384]{2,1,0:T(8,128)(2,1)}, bf16[16,16,640]{2,1,0:T(8,128)(2,1)}, bf16[16,16,128]{2,1,0:T(8,128)(2,1)}) custom-call(bf16[768,256]{1,0:T(8,128)(2,1)} %x_hbm.1, bf16[768,256]{1,0:T(8,128)(2,1)} %c_hbm.1, bf16[768,1152]{1,0:T(8,128)(2,1)} %g_hbm.1, bf16[768,1152]{1,0:T(8,128)(2,1)} %u_hbm.1, bf16[1152,4096]{1,0:T(8,128)(2,1)} %w_hbm.1, ...), custom_call_target="tpu_custom_call" | custom-call | tf_op jit(solution)/shard_map/adapters/pallas_call | solution.py:475
  84.5 2.0 %unpack.1 = (f32[64,256]{1,0:T(8,128)}, f32[64,1152]{1,0:T(8,128)}, f32[64,256]{1,0:T(8,128)}, f32[64,1152]{1,0:T(8,128)}, f32[64,1152]{1,0:T(8,128)}, /*index=5*/f32[64,256]{1,0:T(8,128)}) custom-call(bf16[16,16,384]{2,1,0:T(8,128)(2,1)} %get-tuple-element.15.a_ref, bf16[16,16,640]{2,1,0:T(8,128)(2,1)} %get-tuple-element.16.b_ref, ...), custom_call_target="tpu_custom_call" | custom-call | tf_op jit(solution)/shard_map/unpack/pallas_call | solution.py:487

commit v2 on v1

v2 whole, which is shorter than its diff:
```python
import functools

import jax
import jax.numpy as jnp
from jax import lax
from jax.experimental import pallas as pl
from jax.experimental.pallas import tpu as pltpu
from jax.sharding import PartitionSpec as P

MESH = pl.DeviceIdType.MESH
F32, BF16 = jnp.float32, jnp.bfloat16
CHUNKS = 3
PIECES = 2
DEPTH = 8
SCALE = 2.0
LOW_AT, LAG = (2, 9, 16, 22, 25, 33, 34), 2


def dot_nn(a, b):
    return jnp.dot(a, b, preferred_element_type=F32)


def dot_nt(a, b):
    return lax.dot_general(a, b, (((1,), (1,)), ((), ())), preferred_element_type=F32)


def travel_order(hops):
    own = [(0, b, q * PIECES + s) for q in range(CHUNKS) for b in range(2) for s in range(PIECES)]
    events, sent, at = [], [], 0

    def run(event):
        events.append(event)
        hop, b, s = event
        if hop + 1 < hops or (hop + 1 == hops and b == 0):
            sent.append((hop + 1, b, s))

    while own and len(sent) < DEPTH:
        run(own.pop(0))
    while at < len(sent):
        run(sent[at])
        at += 1
        while own and len(sent) - at < DEPTH:
            run(own.pop(0))
    return events


def main_kernel(
    nz, nd,
    x_hbm, c_hbm, g_hbm, u_hbm, w_hbm, ga_hbm, gb_hbm, ua_hbm, ub_hbm, da_hbm, ds_hbm,
    oa_hbm, ob_hbm, oc_hbm,
    cg, wv, gv, uv, act, usl, hid, xin, wf, wd, acc,
    lp, lpr, fsa, fra, tsa, tra, fsb, frb, tsb, trb, lowa, lowb, lowta, lowtb,
    bp, bpr, bsb, brb, esb, erb, bk,
    gs, us, gda, dsec, gg, ug,
    sa, ra, ta, sb, rb, tb, sc, rc, tc,
    in_sem, w_sem, ring_recv, pair_recv, ring_send, pair_send, red_sem, dp_sem, out_sem,
):
    tokens, d_local = x_hbm.shape
    f_local = g_hbm.shape[1]
    rank = gb_hbm.shape[0]
    nt = 2 * nz
    hops = nz // 2
    rows = tokens // CHUNKS
    half = tokens // 2
    part = half // nz
    group = 16 // nd
    early = (CHUNKS - 1) * rows
    short = rows // PIECES

    t_me = lax.axis_index("tensor")
    d_me = lax.axis_index("dp")
    z = t_me // 2
    c = t_me % 2
    way = 1 - 2 * c

    def at_z(offset):
        return lax.rem(z + offset + 2 * nz, nz)

    def block(offset, core):
        return 2 * at_z(offset) + core

    def remote(src, dst, send, recv, **where):
        return pltpu.make_async_remote_copy(
            src_ref=src, dst_ref=dst, send_sem=send, recv_sem=recv, device_id=where, device_id_type=MESH)

    def wait_bytes(ref, sem):
        pltpu.make_async_copy(ref, ref, sem).wait()

    loads = [
        pltpu.make_async_copy(c_hbm, cg.at[t_me], in_sem.at[0]),
        pltpu.make_async_copy(g_hbm, gv, in_sem.at[1]),
        pltpu.make_async_copy(u_hbm, uv, in_sem.at[2]),
        pltpu.make_async_copy(x_hbm, xin, in_sem.at[3]),
        pltpu.make_async_copy(ga_hbm, wd.at[0:rank], in_sem.at[4]),
        pltpu.make_async_copy(ua_hbm, wd.at[rank:2 * rank], in_sem.at[5]),
        pltpu.make_async_copy(ds_hbm, wd.at[3 * rank:4 * rank], in_sem.at[6]),
        pltpu.make_async_copy(gb_hbm, wf.at[0:rank], in_sem.at[7]),
        pltpu.make_async_copy(ub_hbm, wf.at[2 * rank:3 * rank], in_sem.at[8]),
        pltpu.make_async_copy(da_hbm, wf.at[4 * rank:5 * rank], in_sem.at[9]),
    ]
    for copy in loads:
        copy.start()
    w_loads = [
        pltpu.make_async_copy(w_hbm.at[:, k * d_local:(k + 1) * d_local], wv.at[k], w_sem) for k in range(nt)
    ]

    barrier = pltpu.get_barrier_semaphore()
    for k in range(1, nt):
        pl.semaphore_signal(barrier, inc=1, device_id={"tensor": lax.rem(t_me + k, nt)}, device_id_type=MESH)
    for k in range(1, nd):
        pl.semaphore_signal(barrier, inc=1, device_id={"dp": lax.rem(d_me + k, nd)}, device_id_type=MESH)

    zeros = jnp.zeros((rank, f_local), BF16)
    wf[rank:2 * rank] = zeros
    wf[3 * rank:4 * rank] = zeros
    wf[5 * rank:6 * rank] = zeros
    wd[2 * rank:3 * rank] = jnp.zeros((rank, d_local), BF16)
    for r in range(4):
        sa[4 * r + 3, :, d_local:] = jnp.zeros((16, sa.shape[2] - d_local), BF16)
        for k in (1, 3):
            sb[4 * r + k, :, f_local - 640:] = jnp.zeros((16, 1280 - f_local), BF16)
    gs[...] = jnp.zeros_like(gs)
    us[...] = jnp.zeros_like(us)

    loads[0].wait()
    pl.semaphore_wait(barrier, nt + nd - 2)

    def piece(offset, core, q):
        return cg.at[block(offset, core), q * short:(q + 1) * short]

    def core_of(b):
        return c if b == 0 else 1 - c

    def ring_on(hop, b, q):
        src = piece(-way * hop, core_of(b), q)
        remote(src, src, ring_send, ring_recv.at[2 * hop + b, q], tensor=block(way, c)).start()

    def pair_on(hop, b, q):
        src = piece(-way * hop, core_of(b), q)
        slot = 0 if hop == 0 else 2 * hop - 1 + b
        remote(src, src, pair_send, pair_recv.at[slot, q], tensor=2 * z + 1 - c).start()

    def ring_wait(hop, b, q):
        wait_bytes(piece(-way * hop, core_of(b), q), ring_recv.at[2 * (hop - 1) + b, q])

    def pair_wait(hop, b, q):
        slot = 0 if hop == 0 else 2 * hop - 1 + b
        wait_bytes(piece(way * hop, 1 - core_of(b), q), pair_recv.at[slot, q])

    def multiply(hop, q):
        if hop == 0:
            pair = [t_me, 2 * z + 1 - c]
        else:
            pair = [block(-way * hop, c), block(way * hop, 1 - c)]
            if hop < hops:
                pair += [block(-way * hop, 1 - c), block(way * hop, c)]
        at = slice(q * rows, (q + 1) * rows)
        total = dot_nt(cg[pair[0], at], wv[pair[0]])
        for b in pair[1:]:
            total += dot_nt(cg[b, at], wv[b])
        acc[q] = total if hop == 0 else acc[q] + total

    def prepare(q):
        def body(i, carry):
            at = pl.multiple_of(q * rows + i * 16, 16)
            g = gv[pl.ds(at, 16)].astype(F32)
            u = uv[pl.ds(at, 16)].astype(F32)
            s = 0.5 * jnp.tanh(0.5 * g) + 0.5
            a = g * s
            inner = pl.multiple_of(i * 16, 16)
            act[q, pl.ds(inner, 16)] = a
            usl[q, pl.ds(inner, 16)] = u * (s * (1.0 + (g - a)))
            hid[pl.ds(at, 16)] = (a * u).astype(BF16)
            return carry

        lax.fori_loop(0, rows // 16, body, 0)
        here = slice(q * rows, (q + 1) * rows)
        lp[here, :2 * rank] = dot_nt(xin[here], wd[:2 * rank])
        own = cg[t_me, q * rows:(q + 1) * rows]
        lp[here, 2 * rank:] = dot_nt(hid[here], wf[4 * rank:6 * rank]) + SCALE * dot_nt(own, wd[2 * rank:4 * rank])

    def z_steps(full, count, recv, parts, result, base):
        half = count // 2
        part = half // nz
        mine = pl.ds(pl.multiple_of(c * half, 16), half)
        other = pl.ds(pl.multiple_of((1 - c) * half, 16), half)
        slice_rows = pl.ds(pl.multiple_of(c * half + z * part, 16), part)

        def exchange():
            remote(full.at[other], recv, red_sem.at[base], red_sem.at[base + 1], tensor=2 * z + 1 - c).start()

        def scatter():
            wait_bytes(recv, red_sem.at[base + 1])
            recv[...] += full[mine]
            for n, (cols, out_b, in_b) in enumerate(parts):
                for k in range(nz):
                    out_b[k] = recv[k * part:(k + 1) * part, cols].astype(out_b.dtype)
                for k in range(1, nz):
                    to = at_z(k)
                    remote(out_b.at[to], in_b.at[k - 1], red_sem.at[base + 6 + 2 * n], red_sem.at[base + 7 + 2 * n],
                           tensor=2 * to + c).start()

        def gather():
            for n, (cols, out_b, in_b) in enumerate(parts):
                wait_bytes(in_b, red_sem.at[base + 7 + 2 * n])
                total = recv[pl.ds(pl.multiple_of(z * part, 16), part), cols]
                for k in range(nz - 1):
                    total += in_b[k].astype(F32)
                result[slice_rows, cols] = total.astype(BF16)
            for k in range(1, nz):
                remote(result.at[slice_rows], result.at[slice_rows], red_sem.at[base + 2], red_sem.at[base + 3],
                       tensor=block(k, c)).start()

        def share():
            wait_bytes(result.at[0:(nz - 1) * part], red_sem.at[base + 3])
            remote(result.at[mine], result.at[mine], red_sem.at[base + 4], red_sem.at[base + 5],
                   tensor=2 * z + 1 - c).start()

        def finish():
            wait_bytes(result.at[0:half], red_sem.at[base + 5])

        def drain():
            wait_bytes(recv, red_sem.at[base])
            for n, (cols, out_b, in_b) in enumerate(parts):
                wait_bytes(in_b, red_sem.at[base + 6 + 2 * n])
            wait_bytes(result.at[0:(nz - 1) * part], red_sem.at[base + 2])
            wait_bytes(result.at[0:half], red_sem.at[base + 4])

        return exchange, scatter, gather, share, finish, drain

    low_mine = pl.ds(pl.multiple_of(c * half, 16), half)
    low_other = pl.ds(pl.multiple_of((1 - c) * half, 16), half)
    low_rows = pl.ds(pl.multiple_of(c * half + z * part, 16), part)
    low_parts = [(slice(0, 2 * rank), fsa, fra, tsa, tra), (slice(2 * rank, 4 * rank), fsb, frb, tsb, trb)]

    def low_part(offset, cols):
        return lpr[pl.ds(pl.multiple_of(at_z(offset) * part, 16), part), cols]

    def low_exchange():
        remote(lp.at[low_other], lpr, red_sem.at[0], red_sem.at[1], tensor=2 * z + 1 - c).start()

    def low_near():
        wait_bytes(lpr, red_sem.at[1])
        lpr[...] += lp[low_mine]
        for n, (cols, near_out, near_in, _, _) in enumerate(low_parts):
            for k, offset in enumerate((4 * way, way, -2 * way, -way, 2 * way)):
                near_out[k] = low_part(offset, cols).astype(near_out.dtype)
            for step, some in ((way, slice(0, 3)), (-way, slice(3, 5))):
                remote(near_out.at[some], near_in.at[some], red_sem.at[2 + n], red_sem.at[4 + n],
                       tensor=block(step, c)).start()

    def low_far():
        for n, (cols, _, near_in, far_out, far_in) in enumerate(low_parts):
            wait_bytes(near_in, red_sem.at[4 + n])
            up = low_part(3 * way, cols) + near_in[0].astype(F32) + near_in[4].astype(F32)
            down = low_part(-3 * way, cols) + near_in[2].astype(F32)
            far_out[0] = up.astype(far_out.dtype)
            far_out[1] = down.astype(far_out.dtype)
            for k, step in ((0, 3 * way), (1, -3 * way)):
                remote(far_out.at[k], far_in.at[k], red_sem.at[6 + n], red_sem.at[8 + n], tensor=block(step, c)).start()

    def low_spread(result, base):
        for k in range(1, nz):
            remote(result.at[low_rows], result.at[low_rows], red_sem.at[base], red_sem.at[base + 1],
                   tensor=block(k, c)).start()

    def low_share(result, base):
        wait_bytes(result.at[0:(nz - 1) * part], red_sem.at[base + 1])
        remote(result.at[low_mine], result.at[low_mine], red_sem.at[base + 2], red_sem.at[base + 3],
               tensor=2 * z + 1 - c).start()

    def low_sum():
        for n, (cols, _, near_in, _, far_in) in enumerate(low_parts):
            wait_bytes(far_in, red_sem.at[8 + n])
            total = low_part(0, cols) + near_in[1].astype(F32) + near_in[3].astype(F32)
            total += far_in[0].astype(F32) + far_in[1].astype(F32)
            (lowa, lowb)[n][low_rows] = total.astype(BF16)
        low_spread(lowb, 32)

    def low_drain():
        wait_bytes(lpr, red_sem.at[0])
        for n, (_, _, near_in, _, far_in) in enumerate(low_parts):
            wait_bytes(near_in, red_sem.at[2 + n])
            wait_bytes(far_in, red_sem.at[6 + n])
        for result, base in ((lowa, 28), (lowb, 32)):
            wait_bytes(result.at[0:(nz - 1) * part], red_sem.at[base])
            wait_bytes(result.at[0:half], red_sem.at[base + 2])

    def last_scatter():
        share = rows // nt
        for k in range(nt):
            esb[k] = bp[early + k * share:early + (k + 1) * share].astype(BF16)
        for k in range(1, nt):
            to = lax.rem(t_me + k, nt)
            remote(esb.at[to], erb.at[k - 1], red_sem.at[20], red_sem.at[21], tensor=to).start()

    def last_gather():
        share = rows // nt
        mine = pl.ds(pl.multiple_of(early + t_me * share, 16), share)
        wait_bytes(erb, red_sem.at[21])
        total = bp[mine]
        for k in range(nt - 1):
            total += erb[k].astype(F32)
        bk[mine] = total.astype(BF16)
        for k in range(1, nt):
            remote(bk.at[mine], bk.at[mine], red_sem.at[22], red_sem.at[23], tensor=lax.rem(t_me + k, nt)).start()

    def last_finish():
        wait_bytes(bk.at[0:rows - rows // nt], red_sem.at[23])

    def last_drain():
        wait_bytes(erb, red_sem.at[20])
        wait_bytes(bk.at[0:rows - rows // nt], red_sem.at[22])

    def dp_steps(out_b, in_b, total_b, result, base):
        def scatter():
            for k in range(1, nd):
                to = lax.rem(d_me + k, nd)
                remote(out_b.at[pl.ds(to * group, group)], in_b.at[k - 1], dp_sem.at[base], dp_sem.at[base + 1],
                       dp=to).start()

        def gather():
            wait_bytes(in_b, dp_sem.at[base + 1])
            total = out_b[pl.ds(d_me * group, group)].astype(F32)
            for k in range(nd - 1):
                total += in_b[k].astype(F32)
            total_b[...] = total.astype(BF16)
            place = result.at[pl.ds(d_me * group, group)]
            for k in range(1, nd):
                remote(total_b, place, dp_sem.at[base + 2], dp_sem.at[base + 3], dp=lax.rem(d_me + k, nd)).start()
            pltpu.make_async_copy(total_b, place, out_sem.at[base // 4]).start()

        def finish():
            place = result.at[pl.ds(d_me * group, group)]
            pltpu.make_async_copy(total_b, place, out_sem.at[base // 4]).wait()
            wait_bytes(result.at[0:(nd - 1) * group], dp_sem.at[base + 3])
            wait_bytes(in_b, dp_sem.at[base])
            wait_bytes(result.at[0:(nd - 1) * group], dp_sem.at[base + 2])

        return scatter, gather, finish

    backs = z_steps(bp, early, bpr, [(slice(0, 2 * rank), bsb, brb)], bk, 10)
    first_dp = dp_steps(sa, ra, ta, oa_hbm, 0)
    second_dp = dp_steps(sb, rb, tb, ob_hbm, 4)
    third_dp = dp_steps(sc, rc, tc, oc_hbm, 8)

    def use_lows():
        wait_bytes(lowb.at[0:half], red_sem.at[35])
        for q in range(CHUNKS):
            lowtb[q] = jnp.transpose(lowb[q * rows:(q + 1) * rows].astype(F32)).astype(BF16)
        gda[...] = jnp.zeros_like(gda)
        dsec[...] = jnp.zeros_like(dsec)

        def body(q, carry):
            at = pl.ds(pl.multiple_of(q * rows, 16), rows)
            gda[...] += dot_nn(lowtb[q, rank:], hid[at])
            dsec[...] += dot_nn(lowtb[q, :rank], cg[t_me, at])
            return carry

        lax.fori_loop(0, CHUNKS, body, 0)
        third = f_local // 3
        for r in range(4):
            at = slice(16 * r, 16 * r + 16)
            for k in range(3):
                sa[4 * r + k] = gda[at, k * third:(k + 1) * third].astype(BF16)
            sa[4 * r + 3, :, :d_local] = (SCALE * dsec[at]).astype(BF16)
        first_dp[0]()

    def second_gradients():
        low_share(lowa, 28)
        wait_bytes(lowa.at[0:half], red_sem.at[31])
        for q in range(CHUNKS):
            lowta[q] = jnp.transpose(lowa[q * rows:(q + 1) * rows].astype(F32)).astype(BF16)

        def body(q, carry):
            at = pl.ds(pl.multiple_of(q * rows, 16), rows)
            gs[...] += dot_nn(lowta[q, :rank], gg[at])
            us[...] += dot_nn(lowta[q, rank:], ug[at])
            return carry

        lax.fori_loop(0, CHUNKS, body, 0)

    def post(q):
        here = slice(q * rows, (q + 1) * rows)
        lowq = lowb[here]
        width = f_local // 3

        def body(i, carry):
            cols = pl.ds(pl.multiple_of(i * width, 128), width)
            grad = acc[q, :, cols] + dot_nn(lowq, wf[3 * rank:5 * rank, cols])
            gg[here, cols] = (grad * usl[q, :, cols]).astype(BF16)
            ug[here, cols] = (grad * act[q, :, cols]).astype(BF16)
            return carry

        lax.fori_loop(0, 3, body, 0)
        bp[here] = dot_nt(gg[here], wf[:2 * rank]) + dot_nt(ug[here], wf[rank:3 * rank])
        if q == CHUNKS - 2:
            backs[0]()
        if q == CHUNKS - 1:
            last_scatter()

    events = travel_order(hops)
    arrivals = [e for e in events if e[0] > 0]
    count = len(arrivals)
    def take(hop, q):
        for s in range(q * PIECES, (q + 1) * PIECES):
            for b in range(2 if 0 < hop < hops else 1 if hop else 0):
                pair_wait(hop, b, s)
        multiply(hop, q)

    def last_own():
        wait_bytes(wv, w_sem)

    tasks = [(1, last_own)]
    tasks += list(zip(LOW_AT, [
        low_near, low_far, low_sum, lambda: low_share(lowb, 32), use_lows, first_dp[1], lambda: low_spread(lowa, 28)]))
    done = 0
    finished = {}
    for e in events:
        hop, b, s = e
        done += hop > 0
        finished[hop, s // PIECES] = done
    lows_at = LOW_AT[4]
    for (hop, q), at in finished.items():
        ready = at + 1 if hop == 0 else at + LAG
        tasks.append((ready, functools.partial(take, hop, q)))
        if hop == hops:
            ready = max(finished[h, q] for h in range(hops + 1)) + LAG
            at = max(ready, lows_at) + 1 + q if q < CHUNKS - 1 else max(ready, lows_at + CHUNKS, count) + 1
            tasks.append((at, functools.partial(post, q)))
            if q == CHUNKS - 2:
                tasks += [(at + 3, backs[1]), (at + 9, backs[2])]
    tasks.sort(key=lambda t: t[0])

    for q in range(CHUNKS * PIECES):
        pair_on(0, 0, q)
    done, first = 0, True
    for hop, b, s in events:
        if hop == 0:
            if b == 1:
                pair_wait(0, 0, s)
            ring_on(0, b, s)
            continue
        if first:
            for copy in loads[1:]:
                copy.wait()
            for copy in w_loads:
                copy.start()
            for n in range(CHUNKS):
                prepare(n)
            low_exchange()
            first = False
        ring_wait(hop, b, s)
        if hop + 1 < hops or (hop + 1 == hops and b == 0):
            ring_on(hop, b, s)
        pair_on(hop, b, s)
        done += 1
        if tasks and tasks[0][0] <= done:
            tasks.pop(0)[1]()
    while tasks:
        tasks.pop(0)[1]()

    second_gradients()
    for r in range(4):
        at = slice(16 * r, 16 * r + 16)
        for k, full in ((0, gs), (2, us)):
            sb[4 * r + k] = (SCALE * full[at, :640]).astype(BF16)
            sb[4 * r + k + 1, :, :f_local - 640] = (SCALE * full[at, 640:]).astype(BF16)
    second_dp[0]()
    last_gather()
    backs[3]()
    backs[4]()
    back_t = jnp.transpose(bk[:early].astype(F32)).astype(BF16)
    firsts = dot_nn(back_t, xin[:early])
    last_finish()
    back_t = jnp.transpose(bk[early:].astype(F32)).astype(BF16)
    firsts = SCALE * (firsts + dot_nn(back_t, xin[early:]))
    for r in range(4):
        for k in range(2):
            for m in range(2):
                sc[4 * r + 2 * k + m] = firsts[
                    k * rank + 16 * r:k * rank + 16 * r + 16, 128 * m:128 * m + 128].astype(BF16)
    third_dp[0]()
    second_dp[1]()
    low_drain()
    backs[5]()
    last_drain()
    wait_bytes(cg.at[0:2 * hops - 1], ring_send)
    wait_bytes(cg.at[0:2 * hops], pair_send)
    third_dp[1]()
    first_dp[2]()
    second_dp[2]()
    third_dp[2]()


def unpack_kernel(a_ref, b_ref, c_ref, gf, gs, uf, us, gda, dsec):
    f_local = gs.shape[1]
    d_local = gf.shape[1]
    third = f_local // 3
    for r in range(4):
        at = slice(16 * r, 16 * r + 16)
        for k in range(3):
            gda[at, k * third:(k + 1) * third] = a_ref[4 * r + k].astype(F32)
        dsec[at] = a_ref[4 * r + 3, :, :d_local].astype(F32)
        for k, full in ((0, gs), (2, us)):
            full[at, :640] = b_ref[4 * r + k].astype(F32)
            full[at, 640:] = b_ref[4 * r + k + 1, :, :f_local - 640].astype(F32)
        for k, full in ((0, gf), (2, uf)):
            full[at, :128] = c_ref[4 * r + k].astype(F32)
            full[at, 128:] = c_ref[4 * r + k + 1].astype(F32)


def local(nz, nd, inputs, cotangent, gate_pre, up_pre, down_weight, gate_a, gate_b, up_a, up_b, down_a, down_second):
    tokens, d_local = inputs.shape
    f_local = gate_pre.shape[1]
    rank = gate_b.shape[0]
    nt, hops = 2 * nz, nz // 2
    rows, half = tokens // CHUNKS, tokens // 2
    part, group = half // nz, 16 // nd
    wide_a, wide_b, wide_c = f_local // 3, 640, 128
    any_space = pl.BlockSpec(memory_space=pl.ANY)
    vmem, dma = pltpu.VMEM, pltpu.SemaphoreType.DMA

    def dp_buffers(width):
        return [vmem((16, 16, width), BF16), vmem((nd - 1, group, 16, width), BF16), vmem((group, 16, width), BF16)]

    early, wide_low, wide_back = tokens - rows, 4 * rank, 2 * rank
    spread = early // nt

    scratch = [
        vmem((nt, tokens, d_local), BF16),
        vmem((nt, f_local, d_local), BF16),
        vmem((tokens, f_local), BF16),
        vmem((tokens, f_local), BF16),
        vmem((CHUNKS, rows, f_local), F32),
        vmem((CHUNKS, rows, f_local), F32),
        vmem((tokens, f_local), BF16),
        vmem((tokens, d_local), BF16),
        vmem((6 * rank, f_local), BF16),
        vmem((4 * rank, d_local), BF16),
        vmem((CHUNKS, rows, f_local), F32),
        vmem((tokens, wide_low), F32),
        vmem((half, wide_low), F32),
        vmem((5, part, wide_back), BF16),
        vmem((5, part, wide_back), BF16),
        vmem((2, part, wide_back), BF16),
        vmem((2, part, wide_back), BF16),
        vmem((5, part, wide_back), F32),
        vmem((5, part, wide_back), F32),
        vmem((2, part, wide_back), F32),
        vmem((2, part, wide_back), F32),
        vmem((tokens, wide_back), BF16),
        vmem((tokens, wide_back), BF16),
        vmem((CHUNKS, wide_back, rows), BF16),
        vmem((CHUNKS, wide_back, rows), BF16),
        vmem((tokens, wide_back), F32),
        vmem((early // 2, wide_back), F32),
        vmem((nz, spread, wide_back), BF16),
        vmem((nz - 1, spread, wide_back), BF16),
        vmem((nt, rows // nt, wide_back), BF16),
        vmem((nt - 1, rows // nt, wide_back), BF16),
        vmem((tokens, wide_back), BF16),
        vmem((rank, f_local), F32),
        vmem((rank, f_local), F32),
        vmem((rank, f_local), F32),
        vmem((rank, d_local), F32),
        vmem((tokens, f_local), BF16),
        vmem((tokens, f_local), BF16),
        *dp_buffers(wide_a),
        *dp_buffers(wide_b),
        *dp_buffers(wide_c),
        dma((10,)),
        dma,
        dma((2 * hops - 1, CHUNKS * PIECES)),
        dma((2 * hops, CHUNKS * PIECES)),
        dma,
        dma,
        dma((36,)),
        dma((12,)),
        dma((3,)),
    ]
    packed = pl.pallas_call(
        functools.partial(main_kernel, nz, nd),
        out_shape=[jax.ShapeDtypeStruct((16, 16, w), BF16) for w in (wide_a, wide_b, wide_c)],
        in_specs=[any_space] * 11,
        out_specs=[any_space] * 3,
        scratch_shapes=scratch,
        compiler_params=pltpu.CompilerParams(
            collective_id=0, has_side_effects=True, vmem_limit_bytes=56 * 1024 * 1024),
        name="adapters",
    )(inputs, cotangent, gate_pre, up_pre, down_weight, gate_a.T, gate_b, up_a.T, up_b, down_a.T, down_second)
    small = jax.ShapeDtypeStruct((rank, d_local), F32)
    large = jax.ShapeDtypeStruct((rank, f_local), F32)
    gf, gs, uf, us, gda, dsec = pl.pallas_call(
        unpack_kernel, out_shape=[small, large, small, large, large, small], name="unpack")(*packed)
    return gf.T, gs, uf.T, us, gda.T, dsec


def solution(mesh):
    split, rows, columns = P("dp", "tensor"), P("tensor", None), P(None, "tensor")
    return jax.shard_map(
        functools.partial(local, mesh.shape["tensor"] // 2, mesh.shape["dp"]),
        mesh=mesh,
        in_specs=(split, split, split, split, rows, rows, columns, rows, columns, rows, columns),
        out_specs=(rows, columns, rows, columns, rows, columns),
        check_vma=False,
    )
```

time: 86.6 us -> 82.5 us (0.953)
  Pallas kernels: 85.9 us -> 81.1 us
    pallas_call x1, Pallas kernels: 83.9 us -> 79 us  [local(): pl.pallas_call(functools.partial(main_kernel, nz, nd), out_shape=[jax.Sha...]
where the time goes in v2:
time: 82.5 us; the launch traced here: 81.7 us
  Pallas kernels  81.1 us (98%)
    pallas_call x1, Pallas kernels, local(): pl.pallas_call(functools.partial(main_kernel, nz, nd), out_shape=[jax.Sha...  79 us
    pallas_call x1, Pallas kernels, local(): pl.pallas_call(unpack_kernel, out_shape=[small, large, small, large, larg...  2.04 us

profile of v2, /device:TPU:1, one launch (start us, length us, event | category | flops | bytes accessed | tf_op | source)
XLA Modules:
  0.0 81.7 jit_solution(4064775388838639307)
XLA Ops:
  0.6 79.0 %adapters.1 = (bf16[16,16,384]{2,1,0:T(8,128)(2,1)}, bf16[16,16,640]{2,1,0:T(8,128)(2,1)}, bf16[16,16,128]{2,1,0:T(8,128)(2,1)}) custom-call(bf16[768,256]{1,0:T(8,128)(2,1)} %x_hbm.1, bf16[768,256]{1,0:T(8,128)(2,1)} %c_hbm.1, bf16[768,1152]{1,0:T(8,128)(2,1)} %g_hbm.1, bf16[768,1152]{1,0:T(8,128)(2,1)} %u_hbm.1, bf16[1152,4096]{1,0:T(8,128)(2,1)} %w_hbm.1, ...), custom_call_target="tpu_custom_call" | custom-call | tf_op jit(solution)/shard_map/adapters/pallas_call | solution.py:582
  79.7 2.0 %unpack.1 = (f32[64,256]{1,0:T(8,128)}, f32[64,1152]{1,0:T(8,128)}, f32[64,256]{1,0:T(8,128)}, f32[64,1152]{1,0:T(8,128)}, f32[64,1152]{1,0:T(8,128)}, /*index=5*/f32[64,256]{1,0:T(8,128)}) custom-call(bf16[16,16,384]{2,1,0:T(8,128)(2,1)} %get-tuple-element.15.a_ref, bf16[16,16,640]{2,1,0:T(8,128)(2,1)} %get-tuple-element.16.b_ref, ...), custom_call_target="tpu_custom_call" | custom-call | tf_op jit(solution)/shard_map/unpack/pallas_call | solution.py:594

commit v3 on v2

--- a/solution.py
+++ b/solution.py
@@ -13,7 +13,7 @@
 PIECES = 2
 DEPTH = 8
 SCALE = 2.0
-LOW_AT, LAG = (2, 9, 16, 22, 25, 33, 34), 2
+LOW_AT, LAG = (2, 13, 24, 34, 37, 41, 38), 2
 
 
 def dot_nn(a, b):
@@ -429,9 +429,11 @@
             at = max(ready, lows_at) + 1 + q if q < CHUNKS - 1 else max(ready, lows_at + CHUNKS, count) + 1
             tasks.append((at, functools.partial(post, q)))
             if q == CHUNKS - 2:
-                tasks += [(at + 3, backs[1]), (at + 9, backs[2])]
+                tasks.append((at + 3, backs[1]))
     tasks.sort(key=lambda t: t[0])
 
+    for q in range(PIECES):
+        ring_on(0, 0, q)
     for q in range(CHUNKS * PIECES):
         pair_on(0, 0, q)
     done, first = 0, True
@@ -439,7 +441,8 @@
         if hop == 0:
             if b == 1:
                 pair_wait(0, 0, s)
-            ring_on(0, b, s)
+            if b == 1 or s >= PIECES:
+                ring_on(0, b, s)
             continue
         if first:
             for copy in loads[1:]:
@@ -460,6 +463,7 @@
     while tasks:
         tasks.pop(0)[1]()
 
+    backs[2]()
     second_gradients()
     for r in range(4):
         at = slice(16 * r, 16 * r + 16)

time: 82.5 us -> 78.9 us (0.956)
  Pallas kernels: 81.1 us -> 78.2 us
    pallas_call x1, Pallas kernels: 79 us -> 76.1 us  [local(): pl.pallas_call(functools.partial(main_kernel, nz, nd), out_shape=[jax.Sha...]
where the time goes in v3:
time: 78.9 us; the launch traced here: 78.8 us
  Pallas kernels  78.2 us (99%)
    pallas_call x1, Pallas kernels, local(): pl.pallas_call(functools.partial(main_kernel, nz, nd), out_shape=[jax.Sha...  76.1 us
    pallas_call x1, Pallas kernels, local(): pl.pallas_call(unpack_kernel, out_shape=[small, large, small, large, larg...  2.04 us

profile of v3, /device:TPU:1, one launch (start us, length us, event | category | flops | bytes accessed | tf_op | source)
XLA Modules:
  0.0 78.8 jit_solution(10146785879884201483)
XLA Ops:
  0.6 76.1 %adapters.1 = (bf16[16,16,384]{2,1,0:T(8,128)(2,1)}, bf16[16,16,640]{2,1,0:T(8,128)(2,1)}, bf16[16,16,128]{2,1,0:T(8,128)(2,1)}) custom-call(bf16[768,256]{1,0:T(8,128)(2,1)} %x_hbm.1, bf16[768,256]{1,0:T(8,128)(2,1)} %c_hbm.1, bf16[768,1152]{1,0:T(8,128)(2,1)} %g_hbm.1, bf16[768,1152]{1,0:T(8,128)(2,1)} %u_hbm.1, bf16[1152,4096]{1,0:T(8,128)(2,1)} %w_hbm.1, ...), custom_call_target="tpu_custom_call" | custom-call | tf_op jit(solution)/shard_map/adapters/pallas_call | solution.py:586
  76.8 2.0 %unpack.1 = (f32[64,256]{1,0:T(8,128)}, f32[64,1152]{1,0:T(8,128)}, f32[64,256]{1,0:T(8,128)}, f32[64,1152]{1,0:T(8,128)}, f32[64,1152]{1,0:T(8,128)}, /*index=5*/f32[64,256]{1,0:T(8,128)}) custom-call(bf16[16,16,384]{2,1,0:T(8,128)(2,1)} %get-tuple-element.15.a_ref, bf16[16,16,640]{2,1,0:T(8,128)(2,1)} %get-tuple-element.16.b_ref, ...), custom_call_target="tpu_custom_call" | custom-call | tf_op jit(solution)/shard_map/unpack/pallas_call | solution.py:598
